TPU v7x, 32 devices: a whole 2x2x4 slice. The times are simulated.
32 devices in a mesh: take: 4 (over y, x), outer: 4 (over z), inner: 2 (over core).
Axes of the slice: x: 2, y: 2, z: 4, core: 2. Of those that a mesh axis runs over, the one named last changes fastest.
Arguments:
- frames: bfloat16 [16, 4096, 256], P('take', ('outer', 'inner')), may hold values from -6 to 6
- conv_weight: bfloat16 [3, 3, 256, 256], replicated, may hold values from -0.21875 to 0.21875
- conv_bias: float32 [3, 256], replicated, may hold values from -1 to 1
- dilations: int32 [3], replicated, may hold values from 1 to 64, as said below
- head_weight: bfloat16 [256, 128], replicated, may hold values from -0.375 to 0.375
- present: int32 [16, 4096], P('take', ('outer', 'inner')), may hold values 0 or 1
- frame_keep: float32 [16, 4096], P('take', ('outer', 'inner')), may hold values from 0.5 to 1
- channel_params: float32 [3, 64], replicated, may hold values from 0 to 2
- head_cotangent: bfloat16 [16, 4096, 128], P('take', ('outer', 'inner')), may hold values from -6 to 6
Outputs:
- filtered_mean: float32 [16, 64, 4096], P('take', None, ('outer', 'inner'))
- head_grad: float32 [256, 128], replicated
Inputs may be any that keep to these rules, and one draw needn't show every extreme that they name: `dilations`: every dilation is 1 to 64; some layer has exactly 64 and another exactly 1.
All inputs are finite; a program needn't handle non-finite values. No bound on the sum of `present` on one device may be relied on, other than what follows from the above.
Results may differ from a plain program's by a relative error of at most 0.0048.
Values may be sent and summed in bfloat16 or wider, within the bound.
A program may use at most 64 MiB of HBM per device.

v0:
```python
import jax
import jax.numpy as jnp
from jax import lax
from jax.sharding import PartitionSpec as P

STATE = 64
LAYERS = 3
DMAX = 64


def extended_2(block, sides, width):
    for axis, dim in sides:
        count = lax.axis_size(axis)
        forward = [(i, i + 1) for i in range(count - 1)]
        backward = [(target, source) for source, target in forward]
        low = lax.ppermute(
            lax.slice_in_dim(block, block.shape[dim] - width, None, axis=dim), axis, forward
        )
        high = lax.ppermute(lax.slice_in_dim(block, 0, width, axis=dim), axis, backward)
        block = jnp.concatenate([low, block, high], axis=dim)
    return block


def prefix_2(part, axis, combine, identity):
    place = lax.axis_index(axis)
    gathered = jax.tree.map(lambda a: lax.all_gather(a, axis), part)
    state = jax.tree.map(lambda a, e: jnp.zeros_like(a) + jnp.asarray(e, a.dtype), part, identity)

    def one(turn, state):
        return combine(
            state, jax.tree.map(lambda a: lax.dynamic_index_in_dim(a, turn, 0, False), gathered)
        )

    return lax.fori_loop(0, place, one, state)


def combine(early, late):
    a_one, b_one, c_one, e_one, j_one = early
    a_two, b_two, c_two, e_two, j_two = late
    denom = 1.0 + c_one * j_two
    new_a = a_two * a_one / denom
    new_b = a_two * (b_one + c_one * e_two) / denom + b_two
    new_c = a_two * a_two * c_one / denom + c_two
    new_e = a_one * (e_two - j_two * b_one) / denom + e_one
    new_j = a_one * a_one * j_two / denom + j_one
    return (new_a, new_b, new_c, new_e, new_j)


def doubling_prefix(elems, axis):
    length = elems[0].shape[axis]
    result = elems
    offset = 1
    while offset < length:
        moved = []
        for index, item in enumerate(result):
            fill_value = 1.0 if index == 0 else 0.0
            pad_shape = list(item.shape)
            pad_shape[axis] = offset
            fill = jnp.full(pad_shape, fill_value, item.dtype)
            kept = lax.slice_in_dim(item, 0, length - offset, axis=axis)
            moved.append(jnp.concatenate([fill, kept], axis=axis))
        result = combine(tuple(moved), result)
        offset = offset * 2
    return result


def elements(obs, logp, params, present, keep, first):
    rate = params[0][:, None]
    noise = params[1][:, None]
    scale = params[2][:, None]
    trans = jnp.exp(-rate) * keep
    prec = present * scale * jax.nn.softplus(logp)
    denom = 1.0 + noise * prec
    zeros = jnp.zeros_like(obs)
    elem_a = jnp.where(first, zeros, trans / denom)
    elem_b = jnp.where(first, prec * obs / (1.0 + prec), noise * prec * obs / denom)
    elem_c = jnp.where(first, 1.0 / (1.0 + prec), noise / denom)
    elem_e = jnp.where(first, zeros, trans * prec * obs / denom)
    elem_j = jnp.where(first, zeros, trans * trans * prec / denom)
    return (elem_a, elem_b, elem_c, elem_e, elem_j)


def conv_layer(extended, weights, bias, dilation):
    out_len = extended.shape[1] - 2 * DMAX
    acc = jnp.zeros((extended.shape[0], out_len, extended.shape[2]), jnp.float32)
    for tap in range(3):
        piece = lax.dynamic_slice_in_dim(extended, DMAX + (tap - 1) * dilation, out_len, 1)
        acc = acc + jnp.einsum(
            "tfw,wv->tfv", piece, weights[tap], preferred_element_type=jnp.float32
        )
    center = extended[:, DMAX : DMAX + out_len]
    return (center.astype(jnp.float32) + jax.nn.silu(acc + bias[None, None, :])).astype(
        jnp.bfloat16
    )


def per_device(
    frames,
    conv_weight,
    conv_bias,
    dilations,
    head_weight,
    present,
    frame_keep,
    channel_params,
    head_cotangent,
):
    block_len = frames.shape[1]
    position = lax.axis_index(("outer", "inner"))
    hidden = frames
    for layer in range(LAYERS):
        extended = extended_2(hidden, ((("outer", "inner"), 1),), DMAX)
        hidden = conv_layer(extended, conv_weight[layer], conv_bias[layer], dilations[layer])
    head = jnp.einsum("tfw,ws->tsf", hidden, head_weight, preferred_element_type=jnp.float32)
    obs = head[:, :STATE]
    logp = head[:, STATE:]
    places = position * block_len + jnp.arange(block_len, dtype=jnp.int32)
    first = (places == 0)[None, None, :]
    elems = elements(
        obs,
        logp,
        channel_params,
        present.astype(jnp.float32)[:, None, :],
        frame_keep[:, None, :],
        first,
    )
    local = doubling_prefix(elems, 2)
    totals = tuple((item[:, :, -1] for item in local))
    identity = (jnp.ones_like(totals[0]),) + tuple((jnp.zeros_like(item) for item in totals[1:]))
    prefix = prefix_2(totals, ("outer", "inner"), combine, identity)
    final = combine(tuple((item[:, :, None] for item in prefix)), local)
    grad_local = jnp.einsum(
        "tfw,tfs->ws", hidden, head_cotangent, preferred_element_type=jnp.float32
    )
    head_grad = lax.psum(grad_local, ("take", "outer", "inner"))
    return (final[1], head_grad)


def solution(mesh):
    return jax.shard_map(
        per_device,
        mesh=mesh,
        in_specs=(
            P("take", ("outer", "inner"), None),
            P(),
            P(),
            P(),
            P(),
            P("take", ("outer", "inner")),
            P("take", ("outer", "inner")),
            P(),
            P("take", ("outer", "inner"), None),
        ),
        out_specs=(P("take", None, ("outer", "inner")), P()),
        check_vma=False,
    )
```

profile of v0, /device:TPU:0, one launch (start us, length us, event | category | flops | bytes accessed | tf_op | source)
XLA Modules:
  0.0 183.2 jit_solution(7651531762721489423)
XLA Ops:
  8.4 1.3 collective-permute-start.1
  9.7 3.0 %collective-permute-start = (bf16[4,64,256]{2,1,0:T(8,128)(2,1)S(1)}, bf16[4,64,256]{2,1,0:T(8,128)(2,1)S(1)}, u32[]{:S(2)}, u32[]{:S(2)}) collective-permute-start(bf16[4,64,256]{2,1,0:T(8,128)(2,1)S(1)} %get-tuple-element.199), channel_id=1, source_target_pairs={{0,1},{1,2},{2,3},{3,4},{4,5},{5,6},{6,7},{8,9},{9,10},{10,11},{11... | collective-permute-start | bytes 393224 | tf_op jit(solution)/shard_map/ppermute | solution.py:16
  14.3 3.0 %fusion.65 = f32[4,512,256]{2,1,0:T(8,128)} fusion(bf16[4,512,256]{2,1,0:T(8,128)(2,1)} %param.11, bf16[3,3,256,256]{3,2,1,0:T(8,128)(2,1)} %param.12), kind=kOutput, calls=%fused_computation.140 | convolution fusion | flops 268435456 | bytes 3276800 | tf_op jit(solution)/shard_map/tfw,wv->tfv/dot_general | solution.py:88
  26.9 4.6 %collective-permute-start.2 = (bf16[4,64,256]{2,1,0:T(8,128)(2,1)S(1)}, bf16[4,64,256]{2,1,0:T(8,128)(2,1)S(1)}, u32[]{:S(2)}, u32[]{:S(2)}) collective-permute-start(bf16[4,64,256]{2,1,0:T(8,128)(2,1)S(1)} %get-tuple-element.196), channel_id=1, source_target_pairs={{0,1},{1,2},{2,3},{3,4},{4,5},{5,6},{6,7},{8,9},{9,10},{10,11},{11... | collective-permute-start | bytes 393224 | tf_op jit(solution)/shard_map/ppermute | solution.py:16
  33.2 1.5 collective-permute-done.3
  36.4 5.4 %collective-permute-start.4 = (bf16[4,64,256]{2,1,0:T(8,128)(2,1)S(1)}, bf16[4,64,256]{2,1,0:T(8,128)(2,1)S(1)}, u32[]{:S(2)}, u32[]{:S(2)}) collective-permute-start(bf16[4,64,256]{2,1,0:T(8,128)(2,1)S(1)} %get-tuple-element.194), channel_id=1, source_target_pairs={{0,1},{1,2},{2,3},{3,4},{4,5},{5,6},{6,7},{8,9},{9,10},{10,11},{11... | collective-permute-start | bytes 393224 | tf_op jit(solution)/shard_map/ppermute | solution.py:16
  41.8 1.5 collective-permute-start.5
  43.7 1.3 collective-permute-done.5
  45.6 2.0 %add_convert_fusion = bf16[4,512,256]{2,1,0:T(8,128)(2,1)S(1)} fusion(f32[4,512,256]{2,1,0:T(8,128)S(1)} %fusion.10, f32[4,512,256]{2,1,0:T(8,128)S(1)} %fusion.57, bf16[4,512,256]{2,1,0:T(8,128)(2,1)S(1)} %add_convert_fusion.1, f32[256]{0:T(256)S(1)} %bitcast.224, bf16[4,640,256]{2,1,0:T(8,128)(2,1)S(1)} %pad_maximum_fusion.1, s32[]{:T(128)S(6)} %select_n.53, ...), kind=kOutput, calls=%fused_computation.11 | convolution fusion | flops 273678336 | bytes 7472132 | tf_op jit(solution)/shard_map/tfw,wv->tfv/dot_general | solution.py:88
  51.7 1.3 divide_add_fusion.12
  53.0 1.3 divide_add_fusion.11
  54.3 1.3 divide_add_fusion.10
  55.6 1.3 divide_add_fusion.9
  56.9 1.3 divide_add_fusion.8
  58.2 1.4 fusion.36
  62.9 14.2 %all-gather.4 = f32[32,64,1]{1,2,0:T(1,128)S(1)} all-gather(f32[4,64,1]{1,2,0:T(1,128)S(1)} %copy.20), channel_id=6, replica_groups=mesh['take'=4,'outer'=4,'inner'=2] {'outer','inner'}, dimensions={0}, use_global_device_ids=true | all-gather | bytes 9216 | tf_op jit(solution)/shard_map/all_gather | solution.py:26
  77.2 12.7 %all-gather.3 = f32[32,64,1]{1,2,0:T(1,128)S(1)} all-gather(f32[4,64,1]{1,2,0:T(1,128)S(1)} %copy.19), channel_id=5, replica_groups=mesh['take'=4,'outer'=4,'inner'=2] {'outer','inner'}, dimensions={0}, use_global_device_ids=true | all-gather | bytes 9216 | tf_op jit(solution)/shard_map/all_gather | solution.py:26
  90.0 2.4 %fusion.44 = (f32[4,64,512]{2,1,0:T(8,128)S(1)}, f32[4,64,512]{2,1,0:T(8,128)}, f32[4,64,512]{2,1,0:T(8,128)}) fusion(f32[4,64,512]{2,1,0:T(8,128)S(1)} %get-tuple-element.132, f32[4,64,512]{2,1,0:T(8,128)S(1)} %get-tuple-element.130, f32[4,64,256]{2,1,0:T(8,128)} %copy-done.2, f32[4,64,256]{2,1,0:T(8,128)} %slice.353, f32[4,64,256]{2,1,0:T(8,128)S(1)} %slice.375, ...), kind=kLoop, calls=%fused_computation.69 | loop fusion | flops 1703936 | bytes 4456448 | tf_op jit(solution)/shard_map/add | solution.py:44
  92.6 12.7 %all-gather.1 = f32[32,64,1]{1,2,0:T(1,128)S(1)} all-gather(f32[4,64,1]{1,2,0:T(1,128)S(1)} %copy.17), channel_id=3, replica_groups=mesh['take'=4,'outer'=4,'inner'=2] {'outer','inner'}, dimensions={0}, use_global_device_ids=true | all-gather | bytes 9216 | tf_op jit(solution)/shard_map/all_gather | solution.py:26
  106.4 12.7 %all-gather.2 = f32[32,64,1]{1,2,0:T(1,128)S(1)} all-gather(f32[4,64,1]{1,2,0:T(1,128)S(1)} %copy.18), channel_id=4, replica_groups=mesh['take'=4,'outer'=4,'inner'=2] {'outer','inner'}, dimensions={0}, use_global_device_ids=true | all-gather | bytes 9216 | tf_op jit(solution)/shard_map/all_gather | solution.py:26
  120.2 12.7 %all-gather = f32[32,64,1]{1,2,0:T(1,128)S(1)} all-gather(f32[4,64,1]{1,2,0:T(1,128)S(1)} %copy.16), channel_id=2, replica_groups=mesh['take'=4,'outer'=4,'inner'=2] {'outer','inner'}, dimensions={0}, use_global_device_ids=true | all-gather | bytes 9216 | tf_op jit(solution)/shard_map/all_gather | solution.py:26
  133.0 2.2 %divide_add_fusion = f32[4,64,512]{2,1,0:T(8,128)} fusion(f32[4,64,512]{2,1,0:T(8,128)S(1)} %get-tuple-element.131, f32[4,64,512]{2,1,0:T(8,128)} %get-tuple-element.192, f32[4,64,512]{2,1,0:T(8,128)} %get-tuple-element.193, f32[4,64,512]{2,1,0:T(8,128)S(1)} %get-tuple-element.191, f32[4,64]{1,0:T(4,128)S(1)} %get-tuple-element.110, ...), kind=kLoop, calls=%fused_computation.81 | loop fusion | flops 917504 | bytes 2623488 | tf_op jit(solution)/shard_map/add | solution.py:42
  135.2 39.7 %all-reduce.47.cloned.1.call-done = f32[256,128]{1,0:T(8,128)} async-done(((f32[256,128]{1,0:T(8,128)}), f32[256,128]{1,0:T(8,128)}) %all-reduce.47.cloned.1.call-update) | async-done | bytes 131088 | tf_op jit(solution)/shard_map/psum | solution.py:135
  174.8 1.6 copy.37
  (75 shorter events, 20.4 us)
Async XLA Ops:
  7.2 40.5 %copy-start = (bf16[4,512,128]{2,1,0:T(8,128)(2,1)S(1)}, bf16[4,512,128]{2,1,0:T(8,128)(2,1)}, u32[]{:S(2)}) copy-start(bf16[4,512,128]{2,1,0:T(8,128)(2,1)} %param.19) | copy-start | bytes 1572868
  7.2 16.8 %copy-start.1 = (bf16[4,512,256]{2,1,0:T(8,128)(2,1)S(1)}, bf16[4,512,256]{2,1,0:T(8,128)(2,1)}, u32[]{:S(2)}) copy-start(bf16[4,512,256]{2,1,0:T(8,128)(2,1)} %param.11) | copy-start | bytes 3145732
  7.2 10.1 %copy-start.8 = (s32[3]{0:T(128)S(1)}, s32[3]{0:T(128)}, u32[]{:S(2)}) copy-start(s32[3]{0:T(128)} %param.14) | copy-start | bytes 40
  7.2 16.7 %copy-start.7 = (s32[4,512]{1,0:T(4,128)S(1)}, s32[4,512]{1,0:T(4,128)}, u32[]{:S(2)}) copy-start(s32[4,512]{1,0:T(4,128)} %param.16) | copy-start | bytes 24580
  7.2 167.6 %all-reduce.47.cloned.1.call-start = ((), (), s32[]{:S(2)}) async-start(), calls=%async_computation | async-start | bytes 262144 | tf_op jit(solution)/shard_map/psum | solution.py:135
  8.4 15.8 %collective-permute-start.1 = (bf16[4,64,256]{2,1,0:T(8,128)(2,1)S(1)}, bf16[4,64,256]{2,1,0:T(8,128)(2,1)S(1)}, u32[]{:S(2)}, u32[]{:S(2)}) collective-permute-start(bf16[4,64,256]{2,1,0:T(8,128)(2,1)S(1)} %get-tuple-element.198), channel_id=1, source_target_pairs={{1,0},{2,1},{3,2},{4,3},{5,4},{6,5},{7,6},{9,8},{10,9},{11,10},{12... | collective-permute-start | bytes 393224 | tf_op jit(solution)/shard_map/ppermute | solution.py:19
  9.7 14.3 %collective-permute-start = (bf16[4,64,256]{2,1,0:T(8,128)(2,1)S(1)}, bf16[4,64,256]{2,1,0:T(8,128)(2,1)S(1)}, u32[]{:S(2)}, u32[]{:S(2)}) collective-permute-start(bf16[4,64,256]{2,1,0:T(8,128)(2,1)S(1)} %get-tuple-element.199), channel_id=1, source_target_pairs={{0,1},{1,2},{2,3},{3,4},{4,5},{5,6},{6,7},{8,9},{9,10},{10,11},{11... | collective-permute-start | bytes 393224 | tf_op jit(solution)/shard_map/ppermute | solution.py:16
  17.3 6.8 %copy-start.4 = (bf16[3,3,256,256]{3,2,1,0:T(8,128)(2,1)S(1)}, bf16[3,3,256,256]{3,2,1,0:T(8,128)(2,1)}, u32[]{:S(2)}) copy-start(bf16[3,3,256,256]{3,2,1,0:T(8,128)(2,1)} %param.12) | copy-start | bytes 3538948
  24.1 1.6 copy-start.3
  26.9 6.3 %collective-permute-start.2 = (bf16[4,64,256]{2,1,0:T(8,128)(2,1)S(1)}, bf16[4,64,256]{2,1,0:T(8,128)(2,1)S(1)}, u32[]{:S(2)}, u32[]{:S(2)}) collective-permute-start(bf16[4,64,256]{2,1,0:T(8,128)(2,1)S(1)} %get-tuple-element.196), channel_id=1, source_target_pairs={{0,1},{1,2},{2,3},{3,4},{4,5},{5,6},{6,7},{8,9},{9,10},{10,11},{11... | collective-permute-start | bytes 393224 | tf_op jit(solution)/shard_map/ppermute | solution.py:16
  31.4 3.2 %collective-permute-start.3 = (bf16[4,64,256]{2,1,0:T(8,128)(2,1)S(1)}, bf16[4,64,256]{2,1,0:T(8,128)(2,1)S(1)}, u32[]{:S(2)}, u32[]{:S(2)}) collective-permute-start(bf16[4,64,256]{2,1,0:T(8,128)(2,1)S(1)} %get-tuple-element.197), channel_id=1, source_target_pairs={{1,0},{2,1},{3,2},{4,3},{5,4},{6,5},{7,6},{9,8},{10,9},{11,10},{12... | collective-permute-start | bytes 393224 | tf_op jit(solution)/shard_map/ppermute | solution.py:19
  36.4 7.4 %collective-permute-start.4 = (bf16[4,64,256]{2,1,0:T(8,128)(2,1)S(1)}, bf16[4,64,256]{2,1,0:T(8,128)(2,1)S(1)}, u32[]{:S(2)}, u32[]{:S(2)}) collective-permute-start(bf16[4,64,256]{2,1,0:T(8,128)(2,1)S(1)} %get-tuple-element.194), channel_id=1, source_target_pairs={{0,1},{1,2},{2,3},{3,4},{4,5},{5,6},{6,7},{8,9},{9,10},{10,11},{11... | collective-permute-start | bytes 393224 | tf_op jit(solution)/shard_map/ppermute | solution.py:16
  41.8 3.2 %collective-permute-start.5 = (bf16[4,64,256]{2,1,0:T(8,128)(2,1)S(1)}, bf16[4,64,256]{2,1,0:T(8,128)(2,1)S(1)}, u32[]{:S(2)}, u32[]{:S(2)}) collective-permute-start(bf16[4,64,256]{2,1,0:T(8,128)(2,1)S(1)} %get-tuple-element.195), channel_id=1, source_target_pairs={{1,0},{2,1},{3,2},{4,3},{5,4},{6,5},{7,6},{9,8},{10,9},{11,10},{12... | collective-permute-start | bytes 393224 | tf_op jit(solution)/shard_map/ppermute | solution.py:19
  45.6 3.2 %copy-start.5 = (bf16[256,128]{1,0:T(8,128)(2,1)S(1)}, bf16[256,128]{1,0:T(8,128)(2,1)}, u32[]{:S(2)}) copy-start(bf16[256,128]{1,0:T(8,128)(2,1)} %param.15) | copy-start | bytes 196612
  48.8 1.0 copy-start.6
  60.6 1.3 copy-start.2
Sparse Core Ops, SparseCore 0:
  49.4 125.3 all-reduce.46
where the time goes:
time: 184 us; the launch traced here: 183 us
  blocking collectives  65 us (35%)
  waiting for transfers between devices  42.5 us (23%)
  between operations  20.4 us (11%)
  other arithmetic  17.3 us (9%)
  starting transfers between devices  17.1 us (9%)
  matrix products  11.1 us (6%)
  local copies, waits for them, and re-layouts  9.74 us (5%)
    all_gather x5, blocking collectives, prefix_2(): gathered = jax.tree.map(lambda a: lax.all_gather(a, axis), part)  65 us
    psum x1, waiting for transfers between devices, per_device(): head_grad = lax.psum(grad_local, ('take', 'outer', 'inner'))  39.7 us
    ppermute x3, starting transfers between devices, extended_2(): lax.ppermute(lax.slice_in_dim(block, block.shape[dim] - width, None, axis...  13 us
    add x9, other arithmetic, combine(): new_c = a_two * a_two * c_one / denom + c_two  10 us
    dot_general x9, matrix products, conv_layer(): jnp.einsum('tfw,wv->tfv', piece, weights[tap], preferred_element_type=jnp...  9.51 us
    ppermute x3, starting transfers between devices, extended_2(): lax.ppermute(lax.slice_in_dim(block, 0, width, axis=dim), axis, backward)  4.06 us
  transfers between devices with their start and end apart: 7, of which 3 were waited for; matrix products, arithmetic and copies ran while one was open for 15% of the time, Pallas kernels for 0%

commit v1 on v0

v1 whole, which is shorter than its diff:
```python
import jax
import jax.numpy as jnp
from jax import lax
from jax.experimental import pallas as pl
from jax.experimental.pallas import tpu as pltpu
from jax.sharding import PartitionSpec as P

STATE = 64
WIDTH = 256
LAYERS = 3
DMAX = 64
HALO = 144
PAD = 192
LANES = 128
MESH = pl.DeviceIdType.MESH
F32 = jnp.float32
BF16 = jnp.bfloat16


def recip(x):
    guess = pl.reciprocal(x, approx=True)
    return guess * (2.0 - x * guess)


def combine(early, late):
    a_one, b_one, c_one, e_one, j_one = early
    a_two, b_two, c_two, e_two, j_two = late
    inv = recip(1.0 + c_one * j_two)
    a_inv = a_two * inv
    back = a_one * inv
    return (
        a_inv * a_one,
        a_inv * (b_one + c_one * e_two) + b_two,
        a_two * a_inv * c_one + c_two,
        back * (e_two - j_two * b_one) + e_one,
        a_one * back * j_two + j_one,
    )


def apply(mean, cov, late):
    a_two, b_two, c_two, e_two, j_two = late
    inv = recip(1.0 + cov * j_two)
    a_inv = a_two * inv
    return a_inv * (mean + cov * e_two) + b_two, a_two * a_inv * cov + c_two


def make_kernel(sizes, takes, block):
    n_take, n_outer, n_inner = sizes
    n_time = n_outer * n_inner
    n_plane = n_take * n_inner
    chunk = WIDTH // n_plane
    pairs = takes // 2
    span = block // 8
    groups = span // 8
    rows = block + 2 * PAD

    def kernel(
        dil, frames, weight, bias, head_w, present, keep, params, cot,
        out, grad_out,
        stage, edge, wv, cv, h0, h1, h2, h3, hw2, pk,
        y_s, r_s, f_s, m_s, tot, grad, g_in, g_mid, g_fin,
        load_sem, halo_send, halo_recv, tot_send, tot_recv,
        a_send, a_recv, b_send, b_recv, c_send, c_recv,
    ):
        take = lax.axis_index("take")
        outer = lax.axis_index("outer")
        inner = lax.axis_index("inner")
        pos = outer * n_inner + inner
        mine = take * n_inner + inner

        def time_id(p):
            return {"outer": p // n_inner, "inner": p % n_inner}

        def plane_id(p):
            return {"take": p // n_inner, "inner": p % n_inner}

        def each(count, body):
            def step(j, carry):
                body(j)
                return carry

            lax.fori_loop(1, count, step, 0)

        barrier = pltpu.get_barrier_semaphore()
        each(n_time, lambda j: pl.semaphore_signal(
            barrier, inc=1, device_id=time_id((pos + j) % n_time), device_id_type=MESH))
        each(n_plane, lambda j: pl.semaphore_signal(
            barrier, inc=1, device_id=plane_id((mine + j) % n_plane), device_id_type=MESH))

        loads = [
            pltpu.make_async_copy(frames, stage, load_sem.at[0]),
            pltpu.make_async_copy(weight.at[0], wv.at[0], load_sem.at[1]),
            pltpu.make_async_copy(weight.at[1], wv.at[1], load_sem.at[2]),
            pltpu.make_async_copy(weight.at[2], wv.at[2], load_sem.at[3]),
            pltpu.make_async_copy(cot, cv, load_sem.at[4]),
        ]
        for load in loads:
            load.start()

        pl.semaphore_wait(barrier, n_time - 1 + n_plane - 1)

        to_late = pltpu.make_async_remote_copy(
            src_ref=frames.at[:, pl.ds(block - HALO, HALO), :], dst_ref=edge.at[0],
            send_sem=halo_send.at[0], recv_sem=halo_recv.at[0],
            device_id=time_id(lax.rem(pos + 1, n_time)), device_id_type=MESH)
        to_early = pltpu.make_async_remote_copy(
            src_ref=frames.at[:, pl.ds(0, HALO), :], dst_ref=edge.at[1],
            send_sem=halo_send.at[1], recv_sem=halo_recv.at[1],
            device_id=time_id(lax.rem(pos + n_time - 1, n_time)), device_id_type=MESH)
        has_early = pos > 0
        has_late = pos < n_time - 1

        @pl.when(has_late)
        def _():
            to_late.start()

        @pl.when(has_early)
        def _():
            to_early.start()

        lane_row = lax.broadcasted_iota(jnp.int32, (2 * STATE, 4 * STATE), 0)
        lane_col = lax.broadcasted_iota(jnp.int32, (2 * STATE, 4 * STATE), 1)
        for part in range(2):
            goal = jnp.where(lane_row < STATE, lane_row, lane_row + STATE) + part * STATE
            pick = jnp.where(lane_col == goal, 1.0, 0.0).astype(BF16)
            hw2[part * WIDTH:(part + 1) * WIDTH, :] = jnp.dot(
                head_w[...], pick, preferred_element_type=F32).astype(BF16)
        par_row = lax.broadcasted_iota(jnp.int32, (STATE, LANES), 0)
        par_col = lax.broadcasted_iota(jnp.int32, (STATE, LANES), 1)
        twice = jnp.where(par_col % STATE == par_row, 1.0, 0.0).astype(F32)
        par = jnp.dot(params[...], twice, precision=lax.Precision.HIGHEST, preferred_element_type=F32)
        decay = jnp.exp(-par[0:1, :])
        noise = jnp.broadcast_to(par[1:2, :], (8, LANES))
        scale = par[2:3, :]

        pk[0:takes, :] = keep[...]
        pk[takes:2 * takes, :] = present[...].astype(F32)
        sel_row = lax.broadcasted_iota(jnp.int32, (2 * takes, LANES), 0)
        sel_col = lax.broadcasted_iota(jnp.int32, (2 * takes, LANES), 1)
        frame_row = lax.broadcasted_iota(jnp.int32, (block, LANES), 0)
        start = (frame_row == 0) & (pos == 0)
        for p in range(pairs):
            which = 2 * p + sel_col // STATE
            for base, dest in ((0, f_s), (takes, r_s)):
                pick = jnp.where(sel_row == base + which, 1.0, 0.0).astype(F32)
                wide = lax.dot_general(
                    pk[...], pick, (((0,), (0,)), ((), ())),
                    precision=lax.Precision.HIGHEST, preferred_element_type=F32)
                if base == 0:
                    dest[p] = jnp.where(start, 0.0, wide * decay)
                else:
                    dest[p] = wide * scale

        loads[0].wait()
        for t in range(takes):
            for half in range(2):
                cols = slice(half * LANES, (half + 1) * LANES)
                h0[half, t, PAD:PAD + block, :] = stage[t, :, cols].astype(F32)
                blank = jnp.zeros((PAD - HALO, LANES), F32)
                h0[half, t, 0:PAD - HALO, :] = blank
                h0[half, t, rows - PAD + HALO:rows, :] = blank

        def conv(layer, src, dst, low, high):
            d = dil[layer]
            size = high - low

            def one(t, carry):
                pieces = []
                for tap in range(3):
                    first = PAD + low + (tap - 1) * d if tap != 1 else PAD + low
                    for half in range(2):
                        pieces.append(src[half, t, pl.ds(first, size), :].astype(BF16))
                acc = jnp.dot(
                    jnp.concatenate(pieces, axis=1), wv[layer], preferred_element_type=F32)
                for half in range(2):
                    cols = slice(half * LANES, (half + 1) * LANES)
                    z = 0.5 * (acc[:, cols] + bias[layer:layer + 1, cols])
                    value = src[half, t, PAD + low:PAD + high, :] + (z + z * jnp.tanh(z))
                    value = value.astype(BF16)
                    if layer == LAYERS - 1:
                        dst[t, low:high, cols] = value
                    else:
                        value = value.astype(F32)
                        before, after = max(0, -low), max(0, high - block)
                        if before:
                            dst[half, t, PAD + low:PAD, :] = jnp.where(
                                has_early, value[:before], 0.0)
                        dst[half, t, PAD + low + before:PAD + high - after, :] = value[before:size - after]
                        if after:
                            dst[half, t, PAD + block:PAD + high, :] = jnp.where(
                                has_late, value[size - after:], 0.0)
                return carry

            lax.fori_loop(0, takes, one, 0)

        inside = (DMAX, 2 * DMAX, 3 * DMAX)
        chain = ((h0, h1), (h1, h2), (h2, h3))
        for layer in range(LAYERS):
            loads[1 + layer].wait()
            conv(layer, *chain[layer], inside[layer], block - inside[layer])

        @pl.when(has_early)
        def _():
            to_late.wait_recv()

        @pl.when(has_late)
        def _():
            to_early.wait_recv()

        for t in range(takes):
            for half in range(2):
                cols = slice(half * LANES, (half + 1) * LANES)
                h0[half, t, PAD - HALO:PAD, :] = jnp.where(
                    has_early, edge[0, t, :, cols].astype(F32), 0.0)
                h0[half, t, PAD + block:PAD + block + HALO, :] = jnp.where(
                    has_late, edge[1, t, :, cols].astype(F32), 0.0)
        reach = (2 * DMAX, DMAX, 0)
        for layer in range(LAYERS):
            conv(layer, *chain[layer], -reach[layer], inside[layer])
            conv(layer, *chain[layer], block - inside[layer], block + reach[layer])

        loads[4].wait()
        term = jnp.zeros((WIDTH, 2 * STATE), F32)
        for t in range(takes):
            term = term + lax.dot_general(
                h3[t], cv[t], (((0,), (0,)), ((), ())), preferred_element_type=F32)
        grad[...] = term.reshape(n_plane, chunk, 2 * STATE)

        def a_copy(target, slot, j):
            return pltpu.make_async_remote_copy(
                src_ref=grad.at[target], dst_ref=g_in.at[slot],
                send_sem=a_send.at[j], recv_sem=a_recv.at[slot],
                device_id=plane_id(target), device_id_type=MESH)

        each(n_plane, lambda j: a_copy((mine + j) % n_plane, mine, j).start())

        for p in range(pairs):
            both = jnp.concatenate([h3[2 * p], h3[2 * p + 1]], axis=1)
            head = jnp.dot(both, hw2[...], preferred_element_type=F32)
            y_s[p] = head[:, :LANES]
            logp = head[:, LANES:]
            soft = jnp.maximum(logp, 0.0) + jnp.log1p(jnp.exp(-jnp.abs(logp)))
            r_s[p] = r_s[p] * soft

        sub = lax.broadcasted_iota(jnp.int32, (8, LANES), 0)
        noise_first = jnp.where((sub == 0) & (pos == 0), 1.0, noise)

        def fields(p, g, i):
            where = pl.ds(g * 8 + i, 8, stride=span)
            q = noise_first if (g == 0 and i == 0) else noise
            return y_s.at[p][where, :], r_s.at[p][where, :], f_s.at[p][where, :], q

        tot[pos] = jnp.zeros((16, LANES), F32)
        prefixes, lasts = [], []
        for p in range(pairs):
            chunks = []
            for g in range(groups):
                a = jnp.ones((8, LANES), F32)
                b = c = e = jj = jnp.zeros((8, LANES), F32)
                for i in range(8):
                    y, r, f, q = fields(p, g, i)
                    a_p = f * a
                    c_p = f * f * c + q
                    b_p = f * b
                    inv = recip(1.0 + r * c_p)
                    gain = r * inv
                    push = gain * (y - b_p)
                    a = a_p * inv
                    c = c_p * inv
                    b = b_p + c_p * push
                    e = e + a_p * push
                    jj = jj + a_p * (a_p * gain)
                chunks.append((a, b, c, e, jj))
            width = 1
            while width < groups:
                for g in range(groups):
                    if g & width:
                        chunks[g] = combine(chunks[(g // width) * width - 1], chunks[g])
                width *= 2
            whole = chunks[groups - 1]
            width = 1
            while width < 8:
                moved = tuple(
                    jnp.where(sub >= width, pltpu.roll(x, width, 0), 1.0 if k == 0 else 0.0)
                    for k, x in enumerate(whole))
                whole = combine(moved, whole)
                width *= 2
            for k in range(5):
                tot[pos, pl.ds(2 * k + p, 1), :] = whole[k][7:8, :]
            lasts.append(tuple(
                jnp.where(sub >= 1, pltpu.roll(x, 1, 0), 1.0 if k == 0 else 0.0)
                for k, x in enumerate(whole)))
            prefixes.append(chunks)

        def t_copy(target, slot, j):
            return pltpu.make_async_remote_copy(
                src_ref=tot.at[slot], dst_ref=tot.at[slot],
                send_sem=tot_send.at[j], recv_sem=tot_recv.at[slot],
                device_id=time_id(target), device_id_type=MESH)

        each(n_time, lambda j: t_copy((pos + j) % n_time, pos, j).start())

        each(n_plane, lambda j: a_copy(mine, (mine + j) % n_plane, j).wait_recv())
        g_in[mine] = grad[mine]
        share = lax.fori_loop(
            1, n_plane, lambda j, s: s + g_in[j], g_in[0])
        g_mid[outer] = share

        def b_copy(target, slot, j):
            return pltpu.make_async_remote_copy(
                src_ref=g_mid.at[slot], dst_ref=g_mid.at[slot],
                send_sem=b_send.at[j], recv_sem=b_recv.at[slot],
                device_id={"outer": target}, device_id_type=MESH)

        each(n_outer, lambda j: b_copy((outer + j) % n_outer, outer, j).start())

        each(n_time, lambda j: t_copy(pos, (pos + j) % n_time, j).wait_recv())

        def pass_on(k, state):
            late = tuple(tot[k, 2 * f:2 * f + 2, :] for f in range(5))
            mean, cov = apply(*state, late)
            return jnp.where(k < pos, mean, state[0]), jnp.where(k < pos, cov, state[1])

        none = jnp.zeros((2, LANES), F32)
        mean, cov = lax.fori_loop(0, n_time - 1, pass_on, (none, none))

        def second(p):
            m_s0 = jnp.broadcast_to(mean[p:p + 1, :], (8, LANES))
            c_s0 = jnp.broadcast_to(cov[p:p + 1, :], (8, LANES))
            m_b, c_b = apply(m_s0, c_s0, lasts[p])
            for g in range(groups):
                m, c = (m_b, c_b) if g == 0 else apply(m_b, c_b, prefixes[p][g - 1])
                for i in range(8):
                    y, r, f, q = fields(p, g, i)
                    c_p = f * f * c + q
                    m_p = f * m
                    c = c_p * recip(1.0 + r * c_p)
                    m = m_p + (c * r) * (y - m_p)
                    m_s.at[p][pl.ds(g * 8 + i, 8, stride=span), :] = m
            flat = m_s[p].T
            out[2 * p] = flat[:STATE]
            out[2 * p + 1] = flat[STATE:]

        second(0)

        each(n_outer, lambda j: b_copy(outer, (outer + j) % n_outer, j).wait_recv())
        g_fin[mine] = lax.fori_loop(1, n_outer, lambda j, s: s + g_mid[j], g_mid[0])

        def c_copy(target, slot, j):
            return pltpu.make_async_remote_copy(
                src_ref=g_fin.at[slot], dst_ref=g_fin.at[slot],
                send_sem=c_send.at[j], recv_sem=c_recv.at[slot],
                device_id=plane_id(target), device_id_type=MESH)

        each(n_plane, lambda j: c_copy((mine + j) % n_plane, mine, j).start())

        for p in range(1, pairs):
            second(p)

        each(n_plane, lambda j: c_copy(mine, (mine + j) % n_plane, j).wait_recv())
        grad_out[...] = g_fin[...].reshape(WIDTH, 2 * STATE)

        @pl.when(has_late)
        def _():
            to_late.wait_send()

        @pl.when(has_early)
        def _():
            to_early.wait_send()

        each(n_plane, lambda j: a_copy((mine + j) % n_plane, mine, j).wait_send())
        each(n_time, lambda j: t_copy((pos + j) % n_time, pos, j).wait_send())
        each(n_outer, lambda j: b_copy((outer + j) % n_outer, outer, j).wait_send())
        each(n_plane, lambda j: c_copy((mine + j) % n_plane, mine, j).wait_send())

    vmem = pl.BlockSpec(memory_space=pltpu.VMEM)
    smem = pl.BlockSpec(memory_space=pltpu.SMEM)
    hbm = pl.BlockSpec(memory_space=pl.ANY)
    dma = pltpu.SemaphoreType.DMA
    return pl.pallas_call(
        kernel,
        out_shape=(
            jax.ShapeDtypeStruct((takes, STATE, block), F32),
            jax.ShapeDtypeStruct((WIDTH, 2 * STATE), F32),
        ),
        in_specs=[smem, hbm, hbm, vmem, vmem, vmem, vmem, vmem, hbm],
        out_specs=(vmem, vmem),
        scratch_shapes=[
            pltpu.VMEM((takes, block, WIDTH), BF16),
            pltpu.VMEM((2, takes, HALO, WIDTH), BF16),
            pltpu.VMEM((LAYERS, 3 * WIDTH, WIDTH), BF16),
            pltpu.VMEM((takes, block, 2 * STATE), BF16),
            pltpu.VMEM((2, takes, rows, LANES), F32),
            pltpu.VMEM((2, takes, rows, LANES), F32),
            pltpu.VMEM((2, takes, rows, LANES), F32),
            pltpu.VMEM((takes, block, WIDTH), BF16),
            pltpu.VMEM((2 * WIDTH, 4 * STATE), BF16),
            pltpu.VMEM((2 * takes, block), F32),
            pltpu.VMEM((pairs, block, LANES), F32),
            pltpu.VMEM((pairs, block, LANES), F32),
            pltpu.VMEM((pairs, block, LANES), F32),
            pltpu.VMEM((pairs, block, LANES), F32),
            pltpu.VMEM((n_time, 16, LANES), F32),
            pltpu.VMEM((n_plane, chunk, 2 * STATE), F32),
            pltpu.VMEM((n_plane, chunk, 2 * STATE), F32),
            pltpu.VMEM((n_outer, chunk, 2 * STATE), F32),
            pltpu.VMEM((n_plane, chunk, 2 * STATE), F32),
            dma((5,)), dma((2,)), dma((2,)),
            dma((n_time,)), dma((n_time,)),
            dma((n_plane,)), dma((n_plane,)),
            dma((n_outer,)), dma((n_outer,)),
            dma((n_plane,)), dma((n_plane,)),
        ],
        compiler_params=pltpu.CompilerParams(
            collective_id=0, has_side_effects=True, vmem_limit_bytes=48 * 1024 * 1024),
        cost_estimate=pl.CostEstimate(
            flops=4 * 1000 * 1000 * 1000, bytes_accessed=4 * 1000 * 1000, transcendentals=0),
    )


def solution(mesh):
    sizes = (mesh.shape["take"], mesh.shape["outer"], mesh.shape["inner"])

    def per_device(
        frames, conv_weight, conv_bias, dilations, head_weight,
        present, frame_keep, channel_params, head_cotangent,
    ):
        takes, block, width = frames.shape
        call = make_kernel(sizes, takes, block)
        return call(
            dilations, frames, conv_weight.reshape(LAYERS, 3 * width, width), conv_bias,
            head_weight, present, frame_keep, channel_params, head_cotangent)

    return jax.shard_map(
        per_device,
        mesh=mesh,
        in_specs=(
            P("take", ("outer", "inner"), None),
            P(),
            P(),
            P(),
            P(),
            P("take", ("outer", "inner")),
            P("take", ("outer", "inner")),
            P(),
            P("take", ("outer", "inner"), None),
        ),
        out_specs=(P("take", None, ("outer", "inner")), P()),
        check_vma=False,
    )
```

time: 184 us -> 40.4 us (0.22)
  blocking collectives: 65 us -> 0 us
  waiting for transfers between devices: 42.5 us -> 0 us
  Pallas kernels: 0 us -> 30.1 us
  between operations: 20.4 us -> 0.66 us
  other arithmetic: 17.3 us -> 0 us
  starting transfers between devices: 17.1 us -> 0 us
  matrix products: 11.1 us -> 0 us
    all_gather x5 -> x0, blocking collectives: 65 us -> none  [prefix_2(): gathered = jax.tree.map(lambda a: lax.all_gather(a, axis), part)]
    psum x1 -> x0, waiting for transfers between devices: 39.7 us -> none  [per_device(): head_grad = lax.psum(grad_local, ('take', 'outer', 'inner'))]
    pallas_call x0 -> x1, Pallas kernels: none -> 30.1 us  [per_device(): call(dilations, frames, conv_weight.reshape(LAYERS, 3 * width, width), co...]
    ppermute x6 -> x0, starting transfers between devices: 17.1 us -> none  [the longest x3 13 us: extended_2(): lax.ppermute(lax.slice_in_dim(block, block.shape[dim] - width, None, axis...]
    add x13 -> x0, other arithmetic: 15.8 us -> none  [the longest x9 10 us: combine(): new_c = a_two * a_two * c_one / denom + c_two]
    dot_general x11 -> x0, matrix products: 11.1 us -> none  [the longest x9 9.51 us: conv_layer(): jnp.einsum('tfw,wv->tfv', piece, weights[tap], preferred_element_type=jnp...]
    slice x24 -> x0, local copies, waits for them, and re-layouts: 6.96 us -> none  [the longest x9 2.64 us: per_device(): totals = tuple((item[:, :, -1] for item in local))]
    unnamed x21 -> x20, local copies, waits for them, and re-layouts: 2.77 us -> 9.23 us
  transfers between devices with their start and end apart: 7 -> 0, of which waited for: 3 -> 0; matrix products, arithmetic and copies ran while one was open for 15% -> 0% of each run, Pallas kernels for 0% -> 0%
where the time goes in v1:
time: 40.4 us; the launch traced here: 39.9 us
  Pallas kernels  30.1 us (75%)
  local copies, waits for them, and re-layouts  9.23 us (23%)
  between operations  0.66 us (2%)
    pallas_call x1, Pallas kernels, per_device(): call(dilations, frames, conv_weight.reshape(LAYERS, 3 * width, width), co...  30.1 us
    unnamed x20, local copies, waits for them, and re-layouts  9.23 us

profile of v1, /device:TPU:0, one launch (start us, length us, event | category | flops | bytes accessed | tf_op | source)
XLA Modules:
  0.0 39.9 jit_solution(5708350492732564934)
XLA Ops:
  0.6 0.0 copy-start
  0.6 1.3 %copy-done = bf16[3,3,256,256]{3,2,1,0:T(8,128)(2,1)S(1)} copy-done((bf16[3,3,256,256]{3,2,1,0:T(8,128)(2,1)S(1)}, bf16[3,3,256,256]{3,2,1,0:T(8,128)(2,1)}, u32[]{:S(2)}) %copy-start) | copy-done | bytes 1179672
  1.9 0.0 copy-start.1
  1.9 1.2 %copy-done.1 = bf16[4,512,256]{2,1,0:T(8,128)(2,1)S(1)} copy-done((bf16[4,512,256]{2,1,0:T(8,128)(2,1)S(1)}, bf16[4,512,256]{2,1,0:T(8,128)(2,1)}, u32[]{:S(2)}) %copy-start.1) | copy-done | bytes 1048600
  3.1 0.0 copy-start.2
  3.1 1.0 %copy-done.2 = bf16[4,512,128]{2,1,0:T(8,128)(2,1)S(1)} copy-done((bf16[4,512,128]{2,1,0:T(8,128)(2,1)S(1)}, bf16[4,512,128]{2,1,0:T(8,128)(2,1)}, u32[]{:S(2)}) %copy-start.2) | copy-done | bytes 524312
  4.2 0.0 copy-start.3
  4.2 0.8 %copy-done.3 = bf16[256,128]{1,0:T(8,128)(2,1)S(1)} copy-done((bf16[256,128]{1,0:T(8,128)(2,1)S(1)}, bf16[256,128]{1,0:T(8,128)(2,1)}, u32[]{:S(2)}) %copy-start.3) | copy-done | bytes 65560
  5.0 0.0 copy-start.4
  5.0 0.7 %copy-done.4 = s32[4,512]{1,0:T(4,128)S(1)} copy-done((s32[4,512]{1,0:T(4,128)S(1)}, s32[4,512]{1,0:T(4,128)}, u32[]{:S(2)}) %copy-start.4) | copy-done | bytes 8216
  5.7 0.0 copy-start.5
  5.7 0.7 %copy-done.5 = f32[4,512]{1,0:T(4,128)S(1)} copy-done((f32[4,512]{1,0:T(4,128)S(1)}, f32[4,512]{1,0:T(4,128)}, u32[]{:S(2)}) %copy-start.5) | copy-done | bytes 8216
  6.4 0.0 copy-start.6
  6.4 0.7 %copy-done.6 = f32[3,256]{1,0:T(4,128)S(1)} copy-done((f32[3,256]{1,0:T(4,128)S(1)}, f32[3,256]{1,0:T(4,128)}, u32[]{:S(2)}) %copy-start.6) | copy-done | bytes 3096
  7.1 0.0 copy-start.7
  7.1 0.7 %copy-done.7 = f32[3,64]{1,0:T(4,128)S(1)} copy-done((f32[3,64]{1,0:T(4,128)S(1)}, f32[3,64]{1,0:T(4,128)}, u32[]{:S(2)}) %copy-start.7) | copy-done | bytes 792
  7.8 0.0 copy-start.8
  7.8 0.7 %copy-done.8 = s32[3]{0:T(128)S(1)} copy-done((s32[3]{0:T(128)S(1)}, s32[3]{0:T(128)}, u32[]{:S(2)}) %copy-start.8) | copy-done | bytes 36
  8.4 30.1 %shard_map.104 = (f32[4,64,512]{2,1,0:T(8,128)S(1)}, f32[256,128]{1,0:T(8,128)S(1)}) custom-call(s32[3]{0:T(128)S(1)} %copy-done.8, bf16[4,512,256]{2,1,0:T(8,128)(2,1)S(1)} %copy-done.1, bf16[3,768,256]{2,1,0:T(8,128)(2,1)S(1)} %bitcast.1, f32[3,256]{1,0:T(4,128)S(1)} %copy-done.6, bf16[256,128]{1,0:T(8,128)(2,1)S(1)} %copy-done.3, s32[4,512]{1,0:T(4,128)S(1)} %copy-done.4, ...), custom_call_target="tpu_custom_call" | custom-call | flops 4000000000 | bytes 4000000 | tf_op jit(solution)/shard_map/pallas_call | solution.py:430
  38.5 0.8 %copy.13 = f32[4,64,512]{2,1,0:T(8,128)} copy(f32[4,64,512]{2,1,0:T(8,128)S(1)} %get-tuple-element.4) | data formatting | bytes 1048576
  39.3 0.7 %copy.14 = f32[256,128]{1,0:T(8,128)} copy(f32[256,128]{1,0:T(8,128)S(1)} %get-tuple-element.5) | data formatting | bytes 262144
Async XLA Ops:
  0.6 1.3 %copy-start = (bf16[3,3,256,256]{3,2,1,0:T(8,128)(2,1)S(1)}, bf16[3,3,256,256]{3,2,1,0:T(8,128)(2,1)}, u32[]{:S(2)}) copy-start(bf16[3,3,256,256]{3,2,1,0:T(8,128)(2,1)} %param.10) | copy-start | bytes 3538948
  1.9 1.2 %copy-start.1 = (bf16[4,512,256]{2,1,0:T(8,128)(2,1)S(1)}, bf16[4,512,256]{2,1,0:T(8,128)(2,1)}, u32[]{:S(2)}) copy-start(bf16[4,512,256]{2,1,0:T(8,128)(2,1)} %frames.1) | copy-start | bytes 3145732
  3.1 1.0 %copy-start.2 = (bf16[4,512,128]{2,1,0:T(8,128)(2,1)S(1)}, bf16[4,512,128]{2,1,0:T(8,128)(2,1)}, u32[]{:S(2)}) copy-start(bf16[4,512,128]{2,1,0:T(8,128)(2,1)} %cot.1) | copy-start | bytes 1572868
  4.2 0.8 %copy-start.3 = (bf16[256,128]{1,0:T(8,128)(2,1)S(1)}, bf16[256,128]{1,0:T(8,128)(2,1)}, u32[]{:S(2)}) copy-start(bf16[256,128]{1,0:T(8,128)(2,1)} %head_w.1) | copy-start | bytes 196612
  5.0 0.7 %copy-start.4 = (s32[4,512]{1,0:T(4,128)S(1)}, s32[4,512]{1,0:T(4,128)}, u32[]{:S(2)}) copy-start(s32[4,512]{1,0:T(4,128)} %present.1) | copy-start | bytes 24580
  5.7 0.7 %copy-start.5 = (f32[4,512]{1,0:T(4,128)S(1)}, f32[4,512]{1,0:T(4,128)}, u32[]{:S(2)}) copy-start(f32[4,512]{1,0:T(4,128)} %keep.1) | copy-start | bytes 24580
  6.4 0.7 %copy-start.6 = (f32[3,256]{1,0:T(4,128)S(1)}, f32[3,256]{1,0:T(4,128)}, u32[]{:S(2)}) copy-start(f32[3,256]{1,0:T(4,128)} %bias.1) | copy-start | bytes 9220
  7.1 0.7 %copy-start.7 = (f32[3,64]{1,0:T(4,128)S(1)}, f32[3,64]{1,0:T(4,128)}, u32[]{:S(2)}) copy-start(f32[3,64]{1,0:T(4,128)} %params.1) | copy-start | bytes 2308
  7.8 0.7 %copy-start.8 = (s32[3]{0:T(128)S(1)}, s32[3]{0:T(128)}, u32[]{:S(2)}) copy-start(s32[3]{0:T(128)} %dil.1) | copy-start | bytes 40

commit v2 on v1

--- a/solution.py
+++ b/solution.py
@@ -55,8 +55,9 @@
     rows = block + 2 * PAD
 
     def kernel(
-        dil, frames, weight, bias, head_w, present, keep, params, cot,
+        dil, frames, weight, bias_in, head_in, present_in, keep_in, params_in, cot,
         out, grad_out,
+        bias, head_w, present, keep, params,
         stage, edge, wv, cv, h0, h1, h2, h3, hw2, pk,
         y_s, r_s, f_s, m_s, tot, grad, g_in, g_mid, g_fin,
         load_sem, halo_send, halo_recv, tot_send, tot_recv,
@@ -94,6 +95,14 @@
             pltpu.make_async_copy(weight.at[2], wv.at[2], load_sem.at[3]),
             pltpu.make_async_copy(cot, cv, load_sem.at[4]),
         ]
+        small = [
+            pltpu.make_async_copy(source, target, load_sem.at[5 + k])
+            for k, (source, target) in enumerate((
+                (bias_in, bias), (head_in, head_w), (present_in, present),
+                (keep_in, keep), (params_in, params)))
+        ]
+        for load in small:
+            load.start()
         for load in loads:
             load.start()
 
@@ -118,6 +127,8 @@
         def _():
             to_early.start()
 
+        for load in small:
+            load.wait()
         lane_row = lax.broadcasted_iota(jnp.int32, (2 * STATE, 4 * STATE), 0)
         lane_col = lax.broadcasted_iota(jnp.int32, (2 * STATE, 4 * STATE), 1)
         for part in range(2):
@@ -133,23 +144,24 @@
         noise = jnp.broadcast_to(par[1:2, :], (8, LANES))
         scale = par[2:3, :]
 
-        pk[0:takes, :] = keep[...]
-        pk[takes:2 * takes, :] = present[...].astype(F32)
-        sel_row = lax.broadcasted_iota(jnp.int32, (2 * takes, LANES), 0)
-        sel_col = lax.broadcasted_iota(jnp.int32, (2 * takes, LANES), 1)
+        left = keep[...]
+        for k in range(3):
+            term = left.astype(BF16).astype(F32)
+            pk[k * takes:(k + 1) * takes, :] = term
+            left = left - term
+        pk[3 * takes:4 * takes, :] = present[...].astype(F32)
+        sel_row = lax.broadcasted_iota(jnp.int32, (4 * takes, 2 * pairs * LANES), 0)
+        sel_col = lax.broadcasted_iota(jnp.int32, (4 * takes, 2 * pairs * LANES), 1)
+        same = sel_row % takes == sel_col // STATE % takes
+        is_keep = (sel_row < 3 * takes) == (sel_col < pairs * LANES)
+        pick = jnp.where(same & is_keep, 1.0, 0.0).astype(BF16)
+        wide = lax.dot_general(
+            pk[...].astype(BF16), pick, (((0,), (0,)), ((), ())), preferred_element_type=F32)
         frame_row = lax.broadcasted_iota(jnp.int32, (block, LANES), 0)
         start = (frame_row == 0) & (pos == 0)
         for p in range(pairs):
-            which = 2 * p + sel_col // STATE
-            for base, dest in ((0, f_s), (takes, r_s)):
-                pick = jnp.where(sel_row == base + which, 1.0, 0.0).astype(F32)
-                wide = lax.dot_general(
-                    pk[...], pick, (((0,), (0,)), ((), ())),
-                    precision=lax.Precision.HIGHEST, preferred_element_type=F32)
-                if base == 0:
-                    dest[p] = jnp.where(start, 0.0, wide * decay)
-                else:
-                    dest[p] = wide * scale
+            f_s[p] = jnp.where(start, 0.0, wide[:, p * LANES:(p + 1) * LANES] * decay)
+            r_s[p] = wide[:, (pairs + p) * LANES:(pairs + p + 1) * LANES] * scale
 
         loads[0].wait()
         for t in range(takes):
@@ -160,44 +172,51 @@
                 h0[half, t, 0:PAD - HALO, :] = blank
                 h0[half, t, rows - PAD + HALO:rows, :] = blank
 
-        def conv(layer, src, dst, low, high):
+        def conv(layer, src, dst, spans):
             d = dil[layer]
-            size = high - low
-
-            def one(t, carry):
-                pieces = []
-                for tap in range(3):
-                    first = PAD + low + (tap - 1) * d if tap != 1 else PAD + low
+
+            def one(duo, carry):
+                parts = [(2 * duo + k, low, high) for k in range(2) for low, high in spans]
+                inputs = []
+                for t, low, high in parts:
+                    pieces = []
+                    for tap in range(3):
+                        first = PAD + low + (tap - 1) * d if tap != 1 else PAD + low
+                        for half in range(2):
+                            pieces.append(src[half, t, pl.ds(first, high - low), :].astype(BF16))
+                    inputs.append(jnp.concatenate(pieces, axis=1))
+                total = jnp.dot(
+                    jnp.concatenate(inputs, axis=0), wv[layer], preferred_element_type=F32)
+                taken = 0
+                for t, low, high in parts:
+                    size = high - low
+                    acc = total[taken:taken + size]
+                    taken += size
                     for half in range(2):
-                        pieces.append(src[half, t, pl.ds(first, size), :].astype(BF16))
-                acc = jnp.dot(
-                    jnp.concatenate(pieces, axis=1), wv[layer], preferred_element_type=F32)
-                for half in range(2):
-                    cols = slice(half * LANES, (half + 1) * LANES)
-                    z = 0.5 * (acc[:, cols] + bias[layer:layer + 1, cols])
-                    value = src[half, t, PAD + low:PAD + high, :] + (z + z * jnp.tanh(z))
-                    value = value.astype(BF16)
-                    if layer == LAYERS - 1:
-                        dst[t, low:high, cols] = value
-                    else:
-                        value = value.astype(F32)
-                        before, after = max(0, -low), max(0, high - block)
-                        if before:
-                            dst[half, t, PAD + low:PAD, :] = jnp.where(
-                                has_early, value[:before], 0.0)
-                        dst[half, t, PAD + low + before:PAD + high - after, :] = value[before:size - after]
-                        if after:
-                            dst[half, t, PAD + block:PAD + high, :] = jnp.where(
-                                has_late, value[size - after:], 0.0)
+                        cols = slice(half * LANES, (half + 1) * LANES)
+                        z = 0.5 * (acc[:, cols] + bias[layer:layer + 1, cols])
+                        value = src[half, t, PAD + low:PAD + high, :] + (z + z * jnp.tanh(z))
+                        value = value.astype(BF16)
+                        if layer == LAYERS - 1:
+                            dst[t, low:high, cols] = value
+                        else:
+                            value = value.astype(F32)
+                            before, after = max(0, -low), max(0, high - block)
+                            if before:
+                                dst[half, t, PAD + low:PAD, :] = jnp.where(
+                                    has_early, value[:before], 0.0)
+                            dst[half, t, PAD + low + before:PAD + high - after, :] = value[before:size - after]
+                            if after:
+                                dst[half, t, PAD + block:PAD + high, :] = jnp.where(
+                                    has_late, value[size - after:], 0.0)
                 return carry
 
-            lax.fori_loop(0, takes, one, 0)
-
-        inside = (DMAX, 2 * DMAX, 3 * DMAX)
-        chain = ((h0, h1), (h1, h2), (h2, h3))
-        for layer in range(LAYERS):
-            loads[1 + layer].wait()
-            conv(layer, *chain[layer], inside[layer], block - inside[layer])
+            lax.fori_loop(0, takes // 2, one, 0)
+
+        loads[1].wait()
+        conv(0, h0, h1, [(DMAX, block - DMAX)])
+        loads[2].wait()
+        conv(1, h1, h2, [(2 * DMAX, block - 2 * DMAX)])
 
         @pl.when(has_early)
         def _():
@@ -214,10 +233,10 @@
                     has_early, edge[0, t, :, cols].astype(F32), 0.0)
                 h0[half, t, PAD + block:PAD + block + HALO, :] = jnp.where(
                     has_late, edge[1, t, :, cols].astype(F32), 0.0)
-        reach = (2 * DMAX, DMAX, 0)
-        for layer in range(LAYERS):
-            conv(layer, *chain[layer], -reach[layer], inside[layer])
-            conv(layer, *chain[layer], block - inside[layer], block + reach[layer])
+        conv(0, h0, h1, [(-2 * DMAX, DMAX), (block - DMAX, block + 2 * DMAX)])
+        conv(1, h1, h2, [(-DMAX, 2 * DMAX), (block - 2 * DMAX, block + DMAX)])
+        loads[3].wait()
+        conv(2, h2, h3, [(0, block)])
 
         loads[4].wait()
         term = jnp.zeros((WIDTH, 2 * STATE), F32)
@@ -383,9 +402,14 @@
             jax.ShapeDtypeStruct((takes, STATE, block), F32),
             jax.ShapeDtypeStruct((WIDTH, 2 * STATE), F32),
         ),
-        in_specs=[smem, hbm, hbm, vmem, vmem, vmem, vmem, vmem, hbm],
+        in_specs=[smem] + [hbm] * 8,
         out_specs=(vmem, vmem),
         scratch_shapes=[
+            pltpu.VMEM((LAYERS, WIDTH), F32),
+            pltpu.VMEM((WIDTH, 2 * STATE), BF16),
+            pltpu.VMEM((takes, block), jnp.int32),
+            pltpu.VMEM((takes, block), F32),
+            pltpu.VMEM((3, STATE), F32),
             pltpu.VMEM((takes, block, WIDTH), BF16),
             pltpu.VMEM((2, takes, HALO, WIDTH), BF16),
             pltpu.VMEM((LAYERS, 3 * WIDTH, WIDTH), BF16),
@@ -395,7 +419,7 @@
             pltpu.VMEM((2, takes, rows, LANES), F32),
             pltpu.VMEM((takes, block, WIDTH), BF16),
             pltpu.VMEM((2 * WIDTH, 4 * STATE), BF16),
-            pltpu.VMEM((2 * takes, block), F32),
+            pltpu.VMEM((4 * takes, block), F32),
             pltpu.VMEM((pairs, block, LANES), F32),
             pltpu.VMEM((pairs, block, LANES), F32),
             pltpu.VMEM((pairs, block, LANES), F32),
@@ -405,14 +429,14 @@
             pltpu.VMEM((n_plane, chunk, 2 * STATE), F32),
             pltpu.VMEM((n_outer, chunk, 2 * STATE), F32),
             pltpu.VMEM((n_plane, chunk, 2 * STATE), F32),
-            dma((5,)), dma((2,)), dma((2,)),
+            dma((10,)), dma((2,)), dma((2,)),
             dma((n_time,)), dma((n_time,)),
             dma((n_plane,)), dma((n_plane,)),
             dma((n_outer,)), dma((n_outer,)),
             dma((n_plane,)), dma((n_plane,)),
         ],
         compiler_params=pltpu.CompilerParams(
-            collective_id=0, has_side_effects=True, vmem_limit_bytes=48 * 1024 * 1024),
+            collective_id=0, has_side_effects=True, vmem_limit_bytes=62 * 1024 * 1024),
         cost_estimate=pl.CostEstimate(
             flops=4 * 1000 * 1000 * 1000, bytes_accessed=4 * 1000 * 1000, transcendentals=0),
     )

time: 40.4 us -> 32.5 us (0.80)
  local copies, waits for them, and re-layouts: 9.23 us -> 3.44 us
  Pallas kernels: 30.1 us -> 28.2 us
    unnamed x20 -> x2, local copies, waits for them, and re-layouts: 9.23 us -> 3.44 us
    pallas_call x1, Pallas kernels: 30.1 us -> 28.2 us  [per_device(): call(dilations, frames, conv_weight.reshape(LAYERS, 3 * width, width), co...]
where the time goes in v2:
time: 32.5 us; the launch traced here: 32.3 us
  Pallas kernels  28.2 us (87%)
  local copies, waits for them, and re-layouts  3.44 us (11%)
  between operations  0.64 us (2%)
    pallas_call x1, Pallas kernels, per_device(): call(dilations, frames, conv_weight.reshape(LAYERS, 3 * width, width), co...  28.2 us
    unnamed x2, local copies, waits for them, and re-layouts  3.44 us

profile of v2, /device:TPU:0, one launch (start us, length us, event | category | flops | bytes accessed | tf_op | source)
XLA Modules:
  0.0 32.3 jit_solution(1859843766830019894)
XLA Ops:
  0.6 28.2 %shard_map.104 = (f32[4,64,512]{2,1,0:T(8,128)}, f32[256,128]{1,0:T(8,128)}) custom-call(s32[3]{0:T(128)} %dil.1, bf16[4,512,256]{2,1,0:T(8,128)(2,1)} %frames.1, bf16[3,768,256]{2,1,0:T(8,128)(2,1)} %bitcast.1, f32[3,256]{1,0:T(4,128)} %bias_in.1, bf16[256,128]{1,0:T(8,128)(2,1)} %head_in.1, s32[4,512]{1,0:T(4,128)} %present_in.1, f32[4,512]{1,0:T(4,128)} %keep_in.1, ...), custom_call_target="tpu_custom_call" | custom-call | flops 4000000000 | bytes 4000000 | tf_op jit(solution)/shard_map/pallas_call | solution.py:454
  28.8 1.9 %copy.13 = f32[4,64,512]{2,1,0:T(8,128)} copy(f32[4,64,512]{2,1,0:T(8,128)} %get-tuple-element.4) | data formatting | bytes 1048576
  30.7 1.6 %copy.14 = f32[256,128]{1,0:T(8,128)} copy(f32[256,128]{1,0:T(8,128)} %get-tuple-element.5) | data formatting | bytes 262144
